TPU v7x, 512 devices: a whole 4x4x16 slice. The times are simulated.
512 devices in a mesh: shape: 16 (over z_lo, x), query: 32 (over z_hi, y, core).
Axes of the slice: x: 4, y: 4, z: 16 (z_hi: 4, z_lo: 4; z = z_hi * 4 + z_lo), core: 2. Of those that a mesh axis runs over, the one named last changes fastest.
Arguments:
- queries: bfloat16 [16, 4096, 512], P('shape', 'query'), may hold values from -128 to 128
- keys: bfloat16 [16, 1024, 512], P('shape', 'query'), may hold values from -5 to 5
- values: bfloat16 [16, 1024, 512], P('shape', 'query'), may hold values from -6 to 6
- out_weight: bfloat16 [512, 512], replicated, may hold values from -0.25 to 0.25
- out_grad: float32 [16, 4096, 512], P('shape', 'query'), may hold values from -6 to 6
Outputs:
- query_grad: float32 [16, 4096, 512], P('shape', 'query')
- key_grad: float32 [16, 1024, 512], P('shape', 'query')
- value_grad: float32 [16, 1024, 512], P('shape', 'query')
- weight_grad: float32 [512, 512], replicated
All inputs are finite; a program needn't handle non-finite values.
Results may differ from a plain program's by a relative error of at most 0.02.
Values may be sent and summed in bfloat16 or wider, within the bound.
A program may use at most 64 MiB of HBM per device.

v0:
```python
import math
import jax
import jax.numpy as jnp
from jax import lax
from jax.sharding import PartitionSpec as P

HEADS = 8
HEAD = 64


def shards(queries, keys, values, out_weight, out_grad):
    lat_rows = keys.shape[1]
    width = queries.shape[2]
    scale = 1.0 / math.sqrt(HEAD)
    shape_count = lax.axis_size("shape")
    members = lax.axis_size("query")
    query_rows = queries[0]
    grad_b = out_grad[0].astype(jnp.bfloat16)
    d_attn = jnp.einsum("tf,df->td", grad_b, out_weight, preferred_element_type=jnp.float32).astype(
        jnp.bfloat16
    )
    key_all, value_all = (
        lax.all_gather(keys[0], "query", axis=0, tiled=True),
        lax.all_gather(values[0], "query", axis=0, tiled=True),
    )
    grad_list, attn_list, key_list, value_list = ([], [], [], [])
    for head_index in range(HEADS):
        cols = slice(head_index * HEAD, (head_index + 1) * HEAD)
        q_head = query_rows[:, cols]
        key_head = key_all[:, cols]
        value_head = value_all[:, cols]
        scores = jnp.dot(q_head, key_head.T, preferred_element_type=jnp.float32) * scale
        top = jnp.max(scores, axis=1, keepdims=True)
        lse = top + jnp.log(jnp.sum(jnp.exp(scores - top), axis=1, keepdims=True))
        probs = jnp.exp(scores - lse)
        probs_b = probs.astype(jnp.bfloat16)
        attn_b = jnp.dot(probs_b, value_head, preferred_element_type=jnp.float32).astype(
            jnp.bfloat16
        )
        d_head = d_attn[:, cols]
        delta = jnp.sum(
            d_head.astype(jnp.float32) * attn_b.astype(jnp.float32), axis=1, keepdims=True
        )
        d_probs = jnp.dot(d_head, value_head.T, preferred_element_type=jnp.float32)
        d_scores = (probs * (d_probs - delta) * scale).astype(jnp.bfloat16)
        grad_list.append(jnp.dot(d_scores, key_head, preferred_element_type=jnp.float32))
        key_list.append(
            jnp.einsum("tm,td->md", d_scores, q_head, preferred_element_type=jnp.float32)
        )
        value_list.append(
            jnp.einsum("tm,td->md", probs_b, d_head, preferred_element_type=jnp.float32)
        )
        attn_list.append(attn_b)
    query_grad = jnp.concatenate(grad_list, axis=1)
    attn = jnp.concatenate(attn_list, axis=1)
    key_terms = jnp.concatenate(key_list, axis=1).reshape(members, lat_rows, width)
    value_terms = jnp.concatenate(value_list, axis=1).reshape(members, lat_rows, width)
    key_in, value_in = (
        lax.all_to_all(key_terms, "query", split_axis=0, concat_axis=0, tiled=True),
        lax.all_to_all(value_terms, "query", split_axis=0, concat_axis=0, tiled=True),
    )
    key_grad = jnp.sum(key_in, axis=0)
    value_grad = jnp.sum(value_in, axis=0)
    weight_term = jnp.einsum("td,tf->df", attn, grad_b, preferred_element_type=jnp.float32) * (
        1.0 / shape_count
    )
    weight_grad = lax.psum(weight_term, ("shape", "query"))
    return (query_grad[None], key_grad[None], value_grad[None], weight_grad)


def solution(mesh):
    return jax.shard_map(
        shards,
        mesh=mesh,
        in_specs=(
            P("shape", "query", None),
            P("shape", "query", None),
            P("shape", "query", None),
            P(),
            P("shape", "query", None),
        ),
        out_specs=(
            P("shape", "query", None),
            P("shape", "query", None),
            P("shape", "query", None),
            P(),
        ),
        check_vma=False,
    )
```

profile of v0, /device:TPU:1, one launch (start us, length us, event | category | flops | bytes accessed | tf_op | source)
XLA Modules:
  0.0 804.2 jit_solution(14749125188669435958)
XLA Ops:
  7.2 0.7 all-gather.5.cloned.1.call-update
  8.2 1.3 convolution_convert_fusion
  9.5 79.2 %all-gather.5.cloned.1.call-done = bf16[1,1024,512]{2,1,0:T(8,128)(2,1)} async-done(((bf16[1,32,512]{2,1,0:T(8,128)(2,1)}), bf16[1,1024,512]{2,1,0:T(8,128)(2,1)}) %all-gather.5.cloned.1.call-update) | async-done | bytes 1048592 | tf_op jit(solution)/shard_map/all_gather | solution.py:23
  88.7 1.4 fusion.117
  90.1 1.6 fusion.118
  91.6 1.5 fusion.119
  93.1 0.4 fusion.120
  93.8 0.4 fusion.122
  94.6 0.4 fusion.116
  97.0 1.0 convolution_dynamic-update-slice_fusion.7
  98.0 1.0 convolution_dynamic-update-slice_fusion.6
  99.0 1.0 convolution_dynamic-update-slice_fusion.5
  100.0 1.0 convolution_dynamic-update-slice_fusion.4
  101.0 1.0 convolution_dynamic-update-slice_fusion.3
  102.0 1.0 convolution_dynamic-update-slice_fusion.2
  103.0 1.0 convolution_dynamic-update-slice_fusion.1
  104.0 1.0 convolution_dynamic-update-slice_fusion
  105.0 2.9 copy.27
  107.9 7.5 all-to-all-start.1
  115.4 0.7 all-gather.7.cloned.1.call-update
  116.1 140.1 %all-gather.7.cloned.1.call-done = bf16[1,1024,512]{2,1,0:T(8,128)(2,1)} async-done(((bf16[1,32,512]{2,1,0:T(8,128)(2,1)}), bf16[1,1024,512]{2,1,0:T(8,128)(2,1)}) %all-gather.7.cloned.1.call-update) | async-done | bytes 1048592 | tf_op jit(solution)/shard_map/all_gather | solution.py:24
  256.3 1.4 convolution_convert_fusion.2
  257.7 1.3 convolution_convert_fusion.3
  259.1 1.3 convolution_convert_fusion.4
  261.8 1.0 multiply_reduce_fusion
  262.8 0.9 fusion.23
  263.7 0.9 convolution_dynamic-update-slice_fusion.15
  265.0 1.0 convolution_dynamic-update-slice_fusion.14
  266.3 0.9 convolution_dynamic-update-slice_fusion.13
  267.5 1.0 convolution_dynamic-update-slice_fusion.12
  268.8 0.9 convolution_dynamic-update-slice_fusion.11
  270.1 1.0 convolution_dynamic-update-slice_fusion.10
  271.4 0.9 convolution_dynamic-update-slice_fusion.9
  272.6 1.0 convolution_dynamic-update-slice_fusion.8
  273.6 2.9 copy.26
  276.7 7.6 all-to-all-start
  284.8 2.3 convolution_multiply_fusion
  287.4 0.4 convolution_dynamic-update-slice_fusion.22
  288.0 0.4 convolution_dynamic-update-slice_fusion.20
  288.7 0.4 convolution_dynamic-update-slice_fusion.18
  289.3 0.4 convolution_dynamic-update-slice_fusion.16
  289.7 0.7 copy-done.25
  290.4 1.8 copy.28
  292.2 2.4 reduce_sum.179
  294.5 90.0 %all-to-all-done = f32[32,32,512]{2,1,0:T(8,128)} async-done(((f32[32,32,512]{2,1,0:T(8,128)}), f32[32,32,512]{2,1,0:T(8,128)}, u32[]{:S(2)}, u32[]{:S(2)}) %all-to-all-start) | async-done | bytes 2097184 | tf_op jit(solution)/shard_map/all_to_all | solution.py:59
  384.6 2.4 reduce_sum.178
  386.9 408.5 %all-reduce.2.cloned.1.call-done = f32[512,512]{1,0:T(8,128)} async-done(((f32[512,512]{1,0:T(8,128)}), f32[512,512]{1,0:T(8,128)}) %all-reduce.2.cloned.1.call-update) | async-done | bytes 1048592 | tf_op jit(solution)/shard_map/psum | solution.py:67
  795.4 2.3 copy.59
  (134 shorter events, 7.7 us)
Async XLA Ops:
  7.2 84.4 %copy-start.23 = (bf16[1,128,512]{2,1,0:T(8,128)(2,1)S(1)}, bf16[1,128,512]{2,1,0:T(8,128)(2,1)}, u32[]{:S(2)}) copy-start(bf16[1,128,512]{2,1,0:T(8,128)(2,1)} %param.5) | copy-start | bytes 393220
  7.2 81.5 %all-gather.5.cloned.1.call-start = ((), (), s32[]{:S(2)}) async-start(), calls=%async_computation.3 | async-start | bytes 1081344 | tf_op jit(solution)/shard_map/all_gather | solution.py:23
  88.7 4.4 copy-start.1
  90.0 6.9 copy-start.9
  91.6 6.4 copy-start.7
  93.1 5.9 copy-start.5
  93.5 6.5 copy-start.3
  95.0 9.0 %copy-start.11 = (f32[128,1024]{1,0:T(8,128)}, f32[128,1024]{1,0:T(8,128)S(1)}, u32[]{:S(2)}) copy-start(f32[128,1024]{1,0:T(8,128)S(1)} %get-tuple-element.21) | copy-start | bytes 1572868
  95.2 166.2 %copy-start.43 = (f32[128]{0:T(128)}, f32[128]{0:T(128)S(1)}, u32[]{:S(2)}) copy-start(f32[128]{0:T(128)S(1)} %log_add_fusion.7) | copy-start | bytes 1540
  95.5 165.6 %copy-start.44 = (f32[128]{0:T(128)}, f32[128]{0:T(128)S(1)}, u32[]{:S(2)}) copy-start(f32[128]{0:T(128)S(1)} %log_add_fusion.6) | copy-start | bytes 1540
  95.7 165.0 %copy-start.41 = (f32[128]{0:T(128)}, f32[128]{0:T(128)S(1)}, u32[]{:S(2)}) copy-start(f32[128]{0:T(128)S(1)} %log_add_fusion.5) | copy-start | bytes 1540
  97.0 164.8 %copy-start.46 = (f32[128]{0:T(128)}, f32[128]{0:T(128)S(1)}, u32[]{:S(2)}) copy-start(f32[128]{0:T(128)S(1)} %log_add_fusion) | copy-start | bytes 1540
  107.9 168.7 %all-to-all-start.1 = ((f32[32,32,512]{2,1,0:T(8,128)}), f32[32,32,512]{2,1,0:T(8,128)}, u32[]{:S(2)}, u32[]{:S(2)}) async-start(f32[32,32,512]{2,1,0:T(8,128)} %bitcast.63), calls=%async_computation.1 | async-start | bytes 4194304 | tf_op jit(solution)/shard_map/all_to_all | solution.py:60
  115.4 140.9 %all-gather.7.cloned.1.call-start = ((), (), s32[]{:S(2)}) async-start(), calls=%async_computation.4 | async-start | bytes 1081344 | tf_op jit(solution)/shard_map/all_gather | solution.py:24
  256.3 4.1 copy-start.2
  256.3 4.1 copy-start.4
  256.3 4.5 copy-start.6
  256.3 4.8 copy-start.8
  257.7 4.1 copy-start.26
  257.7 3.8 copy-start.10
  259.0 3.7 copy-start.28
  259.1 2.7 copy-start.12
  260.8 2.9 copy-start.32
  261.1 3.6 copy-start.34
  261.5 3.5 copy-start.36
  261.5 3.2 copy-start.45
  261.8 4.2 copy-start.38
  261.8 4.2 copy-start.42
  265.0 3.8 copy-start.13
  266.3 3.8 copy-start.15
  267.5 3.8 copy-start.17
  268.8 3.8 copy-start.19
  268.8 3.5 copy-start.47
  272.6 4.0 copy-start.21
  276.6 8.0 copy-start.27
  276.6 8.0 copy-start.29
  276.6 8.0 copy-start.31
  276.6 8.0 copy-start.33
  276.6 8.0 copy-start.35
  276.6 8.0 copy-start.37
  276.6 8.0 copy-start.39
  276.6 8.0 copy-start.40
  276.7 107.9 %all-to-all-start = ((f32[32,32,512]{2,1,0:T(8,128)}), f32[32,32,512]{2,1,0:T(8,128)}, u32[]{:S(2)}, u32[]{:S(2)}) async-start(f32[32,32,512]{2,1,0:T(8,128)} %bitcast.64), calls=%async_computation | async-start | bytes 4194304 | tf_op jit(solution)/shard_map/all_to_all | solution.py:59
  284.3 3.1 copy-start.14
  284.3 3.5 copy-start.16
  284.3 511.1 %all-reduce.2.cloned.1.call-start = ((), (), s32[]{:S(2)}) async-start(), calls=%async_computation.2 | async-start | bytes 2097152 | tf_op jit(solution)/shard_map/psum | solution.py:67
  284.8 3.2 copy-start.18
  284.8 3.6 copy-start.20
  (5 other events, 8.9 us)
Sparse Core Ops, SparseCore 0:
  11.2 77.4 all-gather.4
  119.4 136.8 all-gather.6
  291.2 504.1 all-reduce.1
where the time goes:
time: 805 us; the launch traced here: 804 us
  waiting for transfers between devices  719 us (89%)
  matrix products  37.1 us (5%)
  starting transfers between devices  15.4 us (2%)
  between operations  14.6 us (2%)
  local copies, waits for them, and re-layouts  11.2 us (1%)
    psum x1, waiting for transfers between devices, shards(): weight_grad = lax.psum(weight_term, ('shape', 'query'))  408 us
    all_gather x1, waiting for transfers between devices, shards(): lax.all_gather(values[0], 'query', axis=0, tiled=True)  140 us
    all_to_all x1, waiting for transfers between devices, shards(): lax.all_to_all(key_terms, 'query', split_axis=0, concat_axis=0, tiled=True)  90 us
    all_gather x1, waiting for transfers between devices, shards(): lax.all_gather(keys[0], 'query', axis=0, tiled=True)  79.2 us
  transfers between devices with their start and end apart: 5, of which 4 were waited for; matrix products, arithmetic and copies ran while one was open for 4% of the time, Pallas kernels for 0%

commit v1 on v0

--- a/solution.py
+++ b/solution.py
@@ -64,7 +64,8 @@
     weight_term = jnp.einsum("td,tf->df", attn, grad_b, preferred_element_type=jnp.float32) * (
         1.0 / shape_count
     )
-    weight_grad = lax.psum(weight_term, ("shape", "query"))
+    inner = lax.psum(weight_term, "query")
+    weight_grad = lax.psum(inner, "shape")
     return (query_grad[None], key_grad[None], value_grad[None], weight_grad)
 
 

time: 805 us -> 891 us (1.11); the launches traced: 804 us -> 881 us
  waiting for transfers between devices: 719 us -> 793 us
    psum x1 -> x2, waiting for transfers between devices: 408 us -> 573 us  [the longest x1 418 us: shards(): inner = lax.psum(weight_term, 'query')]
    all_to_all x1, waiting for transfers between devices: 90 us -> 0.01 us  [shards(): lax.all_to_all(key_terms, 'query', split_axis=0, concat_axis=0, tiled=True)]
  transfers between devices with their start and end apart: 5 -> 6, of which waited for: 4 -> 4; matrix products, arithmetic and copies ran while one was open for 4% -> 4% of each run, Pallas kernels for 0% -> 0%
where the time goes in v1:
time: 891 us; the launch traced here: 881 us
  waiting for transfers between devices  793 us (89%)
  matrix products  40.3 us (5%)
  starting transfers between devices  15.3 us (2%)
  between operations  14.5 us (2%)
  local copies, waits for them, and re-layouts  10.5 us (1%)
    psum x1, waiting for transfers between devices, shards(): inner = lax.psum(weight_term, 'query')  418 us
    psum x1, waiting for transfers between devices, shards(): weight_grad = lax.psum(inner, 'shape')  155 us
    all_gather x1, waiting for transfers between devices, shards(): lax.all_gather(values[0], 'query', axis=0, tiled=True)  140 us
    all_gather x1, waiting for transfers between devices, shards(): lax.all_gather(keys[0], 'query', axis=0, tiled=True)  79.2 us
  transfers between devices with their start and end apart: 6, of which 4 were waited for; matrix products, arithmetic and copies ran while one was open for 4% of the time, Pallas kernels for 0%

profile of v1, /device:TPU:1, one launch (start us, length us, event | category | flops | bytes accessed | tf_op | source)
XLA Modules:
  0.0 880.5 jit_solution(11504680446807620341)
XLA Ops:
  7.2 0.7 all-gather.5.cloned.1.call-update
  8.2 1.3 convolution_convert_fusion
  9.5 79.2 %all-gather.5.cloned.1.call-done = bf16[1,1024,512]{2,1,0:T(8,128)(2,1)} async-done(((bf16[1,32,512]{2,1,0:T(8,128)(2,1)}), bf16[1,1024,512]{2,1,0:T(8,128)(2,1)}) %all-gather.5.cloned.1.call-update) | async-done | bytes 1048592 | tf_op jit(solution)/shard_map/all_gather | solution.py:23
  88.7 1.4 fusion.117
  90.0 1.6 fusion.118
  91.6 1.5 fusion.119
  93.8 0.4 fusion.122
  97.0 1.0 convolution_dynamic-update-slice_fusion.7
  98.0 1.0 convolution_dynamic-update-slice_fusion.6
  99.0 1.0 convolution_dynamic-update-slice_fusion.5
  100.0 1.0 convolution_dynamic-update-slice_fusion.4
  101.0 1.0 convolution_dynamic-update-slice_fusion.3
  102.0 1.0 convolution_dynamic-update-slice_fusion.2
  103.0 1.0 convolution_dynamic-update-slice_fusion.1
  104.0 1.0 convolution_dynamic-update-slice_fusion
  105.0 2.9 copy.27
  107.9 7.5 all-to-all-start.1
  115.4 0.7 all-gather.7.cloned.1.call-update
  116.1 139.8 %all-gather.7.cloned.1.call-done = bf16[1,1024,512]{2,1,0:T(8,128)(2,1)} async-done(((bf16[1,32,512]{2,1,0:T(8,128)(2,1)}), bf16[1,1024,512]{2,1,0:T(8,128)(2,1)}) %all-gather.7.cloned.1.call-update) | async-done | bytes 1048592 | tf_op jit(solution)/shard_map/all_gather | solution.py:24
  255.9 1.4 convolution_convert_fusion.2
  257.3 1.3 convolution_convert_fusion.3
  258.7 1.3 convolution_convert_fusion.4
  261.4 1.0 multiply_reduce_fusion
  262.7 0.9 convolution_dynamic-update-slice_fusion.15
  263.9 1.0 convolution_dynamic-update-slice_fusion.14
  265.2 0.9 convolution_dynamic-update-slice_fusion.13
  266.5 1.0 convolution_dynamic-update-slice_fusion.12
  267.8 0.9 convolution_dynamic-update-slice_fusion.11
  269.1 1.0 convolution_dynamic-update-slice_fusion.10
  270.3 0.9 convolution_dynamic-update-slice_fusion.9
  271.6 1.0 convolution_dynamic-update-slice_fusion.8
  272.6 2.9 copy.26
  275.6 7.6 all-to-all-start
  283.6 1.3 convolution_multiply_fusion
  285.0 0.8 convolution_dynamic-update-slice_fusion.23
  285.8 1.0 convolution_dynamic-update-slice_fusion.22
  286.8 0.8 convolution_dynamic-update-slice_fusion.21
  287.7 417.7 %all-reduce.3.cloned.1.call-done = f32[512,512]{1,0:T(8,128)} async-done(((f32[512,512]{1,0:T(8,128)}), f32[512,512]{1,0:T(8,128)}) %all-reduce.3.cloned.1.call-update) | async-done | bytes 1048592 | tf_op jit(solution)/shard_map/psum | solution.py:67
  705.4 1.0 convolution_dynamic-update-slice_fusion.20
  706.4 0.9 convolution_dynamic-update-slice_fusion.19
  707.3 1.0 convolution_dynamic-update-slice_fusion.18
  708.2 0.8 convolution_dynamic-update-slice_fusion.17
  709.1 1.0 convolution_dynamic-update-slice_fusion.16
  710.1 1.8 copy.28
  711.8 2.4 reduce_sum.179
  714.2 2.4 reduce_sum.178
  716.6 155.1 %all-reduce.5.cloned.1.call-done = f32[512,512]{1,0:T(8,128)} async-done(((f32[512,512]{1,0:T(8,128)}), f32[512,512]{1,0:T(8,128)}) %all-reduce.5.cloned.1.call-update) | async-done | bytes 1048592 | tf_op jit(solution)/shard_map/psum | solution.py:68
  871.7 2.3 copy.60
  (131 shorter events, 7.7 us)
Async XLA Ops:
  7.2 84.4 %copy-start.25 = (bf16[1,128,512]{2,1,0:T(8,128)(2,1)S(1)}, bf16[1,128,512]{2,1,0:T(8,128)(2,1)}, u32[]{:S(2)}) copy-start(bf16[1,128,512]{2,1,0:T(8,128)(2,1)} %param.5) | copy-start | bytes 393220
  7.2 81.5 %all-gather.5.cloned.1.call-start = ((), (), s32[]{:S(2)}) async-start(), calls=%async_computation.4 | async-start | bytes 1081344 | tf_op jit(solution)/shard_map/all_gather | solution.py:23
  88.7 4.4 copy-start.1
  90.0 6.9 copy-start.9
  91.6 6.3 copy-start.7
  93.1 5.9 copy-start.5
  93.5 6.5 copy-start.3
  95.0 9.0 %copy-start.11 = (f32[128,1024]{1,0:T(8,128)}, f32[128,1024]{1,0:T(8,128)S(1)}, u32[]{:S(2)}) copy-start(f32[128,1024]{1,0:T(8,128)S(1)} %get-tuple-element.21) | copy-start | bytes 1572868
  97.0 164.4 %copy-start.43 = (f32[128]{0:T(128)}, f32[128]{0:T(128)S(1)}, u32[]{:S(2)}) copy-start(f32[128]{0:T(128)S(1)} %log_add_fusion) | copy-start | bytes 1540
  107.9 167.7 %all-to-all-start.1 = ((f32[32,32,512]{2,1,0:T(8,128)}), f32[32,32,512]{2,1,0:T(8,128)}, u32[]{:S(2)}, u32[]{:S(2)}) async-start(f32[32,32,512]{2,1,0:T(8,128)} %bitcast.63), calls=%async_computation.1 | async-start | bytes 4194304 | tf_op jit(solution)/shard_map/all_to_all | solution.py:60
  115.4 140.5 %all-gather.7.cloned.1.call-start = ((), (), s32[]{:S(2)}) async-start(), calls=%async_computation.5 | async-start | bytes 1081344 | tf_op jit(solution)/shard_map/all_gather | solution.py:24
  255.9 4.1 copy-start.2
  255.9 4.1 copy-start.4
  255.9 4.5 copy-start.6
  255.9 4.8 copy-start.8
  257.3 4.1 copy-start.28
  257.3 3.7 copy-start.10
  258.7 3.7 copy-start.30
  258.7 2.7 copy-start.12
  260.0 2.3 copy-start.32
  260.4 2.0 copy-start.34
  260.7 1.7 copy-start.36
  262.7 3.8 copy-start.13
  263.6 2.9 copy-start.26
  263.9 3.8 copy-start.17
  265.2 3.8 copy-start.21
  267.8 3.8 copy-start.15
  267.8 3.5 copy-start.44
  269.1 2.5 copy-start.19
  271.6 4.0 copy-start.23
  275.5 7.8 copy-start.29
  275.5 7.8 copy-start.31
  275.6 7.8 copy-start.33
  275.6 7.8 copy-start.35
  275.6 7.8 copy-start.37
  275.6 7.8 copy-start.39
  275.6 7.8 copy-start.41
  275.6 7.8 copy-start.42
  275.6 8.0 copy-start.27
  275.6 438.6 %all-to-all-start = ((f32[32,32,512]{2,1,0:T(8,128)}), f32[32,32,512]{2,1,0:T(8,128)}, u32[]{:S(2)}, u32[]{:S(2)}) async-start(f32[32,32,512]{2,1,0:T(8,128)} %bitcast.64), calls=%async_computation | async-start | bytes 4194304 | tf_op jit(solution)/shard_map/all_to_all | solution.py:59
  283.3 1.7 copy-start.14
  283.3 2.5 copy-start.18
  283.3 3.5 copy-start.22
  283.3 422.1 %all-reduce.3.cloned.1.call-start = ((), (), s32[]{:S(2)}) async-start(), calls=%async_computation.2 | async-start | bytes 2097152 | tf_op jit(solution)/shard_map/psum | solution.py:67
  284.9 421.5 %copy-start.16 = (bf16[128,1024]{1,0:T(8,128)(2,1)S(1)}, bf16[128,1024]{1,0:T(8,128)(2,1)}, u32[]{:S(2)}) copy-start(bf16[128,1024]{1,0:T(8,128)(2,1)} %copy-done.15) | copy-start | bytes 786436
  284.9 422.4 %copy-start.20 = (bf16[128,1024]{1,0:T(8,128)(2,1)S(1)}, bf16[128,1024]{1,0:T(8,128)(2,1)}, u32[]{:S(2)}) copy-start(bf16[128,1024]{1,0:T(8,128)(2,1)} %copy-done.19) | copy-start | bytes 786436
  284.9 586.8 %all-reduce.5.cloned.1.call-start = ((), (), s32[]{:S(2)}) async-start(), calls=%async_computation.3 | async-start | bytes 2097152 | tf_op jit(solution)/shard_map/psum | solution.py:68
  285.8 423.3 %copy-start.24 = (bf16[128,1024]{1,0:T(8,128)(2,1)S(1)}, bf16[128,1024]{1,0:T(8,128)(2,1)}, u32[]{:S(2)}) copy-start(bf16[128,1024]{1,0:T(8,128)(2,1)} %copy-done.23) | copy-start | bytes 786436
  (3 other events, 3.4 us)
Sparse Core Ops, SparseCore 0:
  11.2 77.4 all-gather.4
  119.4 136.5 all-gather.6
  287.6 417.7 all-reduce.2
  708.4 163.2 all-reduce.4
